TPU v7x, 128 devices: a whole 4x4x4 slice. The times are simulated.
128 devices in a mesh: dp: 16 (over x, y), seq: 8 (over z, core).
Axes of the slice: x: 4, y: 4, z: 4, core: 2. Of those that a mesh axis runs over, the one named last changes fastest.
Arguments:
- queries: bfloat16 [16, 8, 384, 1024], P('dp', 'seq'), may hold values from -6 to 6
- keys: bfloat16 [16, 8, 384, 1024], P('dp', 'seq'), may hold values from -6 to 6
- values: bfloat16 [16, 8, 384, 1024], P('dp', 'seq'), may hold values from -6 to 6
- gates: bfloat16 [16, 8, 384, 1024], P('dp', 'seq'), may hold values from -6 to 6
- attended: bfloat16 [16, 8, 384, 1024], P('dp', 'seq')
- out_grad: bfloat16 [16, 8, 384, 1024], P('dp', 'seq'), may hold values from -6 to 6
- plan: int32 [16, 8, 16], P(None, 'seq'), may hold values from 1 to 24, 256 in all within a row
- hist_len: int32 [16], P('dp'), may hold values from 512 to 2048, as said below
- block_mask: int32 [16, 16, 16], P('dp'), may hold values 0 or 1
Outputs:
- query_grad: bfloat16 [16, 8, 384, 1024], P('dp', 'seq')
- key_grad: bfloat16 [16, 8, 384, 1024], P('dp', 'seq')
- value_grad: bfloat16 [16, 8, 384, 1024], P('dp', 'seq')
- gate_grad: bfloat16 [16, 8, 384, 1024], P('dp', 'seq')
Inputs may be any that keep to these rules, and one draw needn't show every extreme that they name: For every history g and piece s, plan[g, s, :] sums to 256; some entry of each such row equals 24. `hist_len`: some history has exactly 2048 events.
All inputs are finite; a program needn't handle non-finite values. No bound on the sum of `block_mask` on one device may be relied on, other than what follows from the above.
Results may differ from a plain program's by a relative error of at most 0.0058.
Values may be sent and summed in bfloat16 or wider, within the bound.
A program may use at most 128 MiB of HBM per device.

v0:
```python
import jax
import jax.numpy as jnp
from jax import lax
from jax.sharding import PartitionSpec as P

HEADS = 8
ROWS = 256
BLOCK = 128


def layer_norm(inputs):
    center = inputs - jnp.mean(inputs, axis=-1, keepdims=True)
    spread = jnp.mean(center * center, axis=-1, keepdims=True)
    return center * lax.rsqrt(spread + 1e-05)


def flatten(array):
    return array.reshape(array.shape[2], array.shape[3])


def cut_rows(array, offset, extent, head_count):
    return array[offset : offset + extent].reshape(extent, head_count, -1)


def pair_terms(query_rows, grad_rows, key_rows, value_rows, live_weight):
    scale_qk = query_rows.shape[2] ** (-0.5)
    scores = (
        jnp.einsum("thd,shd->hts", query_rows, key_rows, preferred_element_type=jnp.float32)
        * scale_qk
    )
    sigmoid = jax.nn.sigmoid(scores)
    weight = (scores * sigmoid * live_weight[None]).astype(jnp.bfloat16)
    products = jnp.einsum("thd,shd->hts", grad_rows, value_rows, preferred_element_type=jnp.float32)
    score_grad = (
        products * (sigmoid * (1.0 + scores * (1.0 - sigmoid))) * live_weight[None]
    ).astype(jnp.bfloat16)
    query_part = (
        jnp.einsum("hts,shd->thd", score_grad, key_rows, preferred_element_type=jnp.float32)
        * scale_qk
    )
    key_part = (
        jnp.einsum("hts,thd->shd", score_grad, query_rows, preferred_element_type=jnp.float32)
        * scale_qk
    )
    value_part = jnp.einsum("hts,thd->shd", weight, grad_rows, preferred_element_type=jnp.float32)
    return (query_part, key_part, value_part)


def local(queries, keys, values, gates, attended, out_grad, plan, hist_len, block_mask):
    group_count = lax.axis_size("dp")
    capacity = queries.shape[2]
    model_width = queries.shape[3]
    slot_count = capacity // group_count
    row_count = ROWS
    head_count = HEADS
    head_size = model_width // head_count
    dp_index = lax.axis_index("dp")
    seq_index = lax.axis_index("seq")
    group_ids = jnp.arange(group_count, dtype=jnp.int32)
    slot_ids = jnp.arange(slot_count, dtype=jnp.int32)
    row_ids = jnp.arange(row_count, dtype=jnp.int32)
    my_plan = plan[:, 0, :]
    incoming = jnp.sum(jnp.where(group_ids[None, :] == dp_index, my_plan, 0), axis=1)
    valid = (slot_ids[None, :] < incoming[:, None]).reshape(capacity)
    normed, pullback = jax.vjp(layer_norm, flatten(attended).astype(jnp.float32))
    cotangent = flatten(out_grad).astype(jnp.float32) * flatten(gates).astype(jnp.float32)
    attn_grad = pullback(cotangent)[0].astype(jnp.bfloat16)
    gate_grad = jnp.where(
        valid[:, None], flatten(out_grad).astype(jnp.float32) * normed, 0.0
    ).astype(jnp.bfloat16)
    shape_slots = (group_count, slot_count, model_width)
    received = (
        lax.all_to_all(
            flatten(queries).reshape(shape_slots), "dp", split_axis=0, concat_axis=0, tiled=True
        ),
        lax.all_to_all(
            flatten(keys).reshape(shape_slots), "dp", split_axis=0, concat_axis=0, tiled=True
        ),
        lax.all_to_all(
            flatten(values).reshape(shape_slots), "dp", split_axis=0, concat_axis=0, tiled=True
        ),
        lax.all_to_all(
            attn_grad.reshape(shape_slots), "dp", split_axis=0, concat_axis=0, tiled=True
        ),
    )
    own_counts = jnp.sum(jnp.where(group_ids[:, None] == dp_index, my_plan, 0), axis=0)
    cum_incl = jnp.cumsum(own_counts)
    cum_excl = cum_incl - own_counts
    dest = jnp.sum((cum_incl[None, :] <= row_ids[:, None]).astype(jnp.int32), axis=1)
    begin = jnp.sum(jnp.where(group_ids[None, :] == dest[:, None], cum_excl[None, :], 0), axis=1)
    flat_index = dest * slot_count + row_ids - begin
    history = []
    for array in received:
        history.append(
            jnp.take(array.reshape(group_count * slot_count, model_width), flat_index, axis=0)
        )
    length = hist_len[0]
    pattern = block_mask[0].astype(jnp.float32)
    block_total = pattern.shape[0]
    inverse = 1.0 / jnp.sqrt(length.astype(jnp.float32))
    block_ids = jnp.arange(block_total, dtype=jnp.int32)

    def live_mask(query_pos, key_pos):
        query_block = query_pos // BLOCK
        key_block = key_pos // BLOCK
        onehot_query = (query_block[:, None] == block_ids[None, :]).astype(jnp.float32)
        onehot_key = (key_block[:, None] == block_ids[None, :]).astype(jnp.float32)
        blocks = jnp.dot(
            jnp.dot(onehot_query, pattern, precision=lax.Precision.HIGHEST),
            onehot_key.T,
            precision=lax.Precision.HIGHEST,
        )
        keep = (
            (key_pos[None, :] <= query_pos[:, None])
            & (query_pos[:, None] < length)
            & (key_pos[None, :] < length)
        )
        keep = keep & ((blocks > 0.5) | (query_block[:, None] == key_block[None, :]))
        return keep.astype(jnp.float32) * inverse

    own_pos = seq_index * row_count + row_ids
    own_query = history[0].reshape(row_count, head_count, head_size)
    own_key = history[1].reshape(row_count, head_count, head_size)
    own_value = history[2].reshape(row_count, head_count, head_size)
    own_grad = history[3].reshape(row_count, head_count, head_size)
    zeros = jnp.zeros((row_count, head_count, head_size), jnp.float32)
    anchor = jnp.int32(0)
    shard_query = lax.all_gather(history[0], "seq", axis=0, tiled=True)
    shard_key = lax.all_gather(history[1], "seq", axis=0, tiled=True)
    shard_value = lax.all_gather(history[2], "seq", axis=0, tiled=True)
    shard_grad = lax.all_gather(history[3], "seq", axis=0, tiled=True)
    total = shard_query.shape[0]
    query_sum = zeros
    key_sum = zeros
    value_sum = zeros
    for offset in range(0, total, 1024):
        extent = min(1024, total - offset)
        positions = anchor + offset + jnp.arange(extent, dtype=jnp.int32)
        part_query = cut_rows(shard_query, offset, extent, head_count)
        part_key = cut_rows(shard_key, offset, extent, head_count)
        part_value = cut_rows(shard_value, offset, extent, head_count)
        part_grad = cut_rows(shard_grad, offset, extent, head_count)
        earlier = pair_terms(
            own_query, own_grad, part_key, part_value, live_mask(own_pos, positions)
        )
        later = pair_terms(part_query, part_grad, own_key, own_value, live_mask(positions, own_pos))
        query_sum = query_sum + earlier[0]
        key_sum = key_sum + later[1]
        value_sum = value_sum + later[2]
    sums = (query_sum, key_sum, value_sum)
    grads = [array.astype(jnp.bfloat16).reshape(row_count, model_width) for array in sums]
    row_index = jnp.minimum(cum_excl[:, None] + slot_ids[None, :], row_count - 1).reshape(-1)
    keep_slots = (slot_ids[None, :] < own_counts[:, None]).reshape(-1)

    def pack(array):
        picked = jnp.take(array, row_index, axis=0)
        return jnp.where(keep_slots[:, None], picked, 0.0).reshape(shape_slots)

    returned = (
        lax.all_to_all(pack(grads[0]), "dp", split_axis=0, concat_axis=0, tiled=True),
        lax.all_to_all(pack(grads[1]), "dp", split_axis=0, concat_axis=0, tiled=True),
        lax.all_to_all(pack(grads[2]), "dp", split_axis=0, concat_axis=0, tiled=True),
    )
    out_shape = (1, 1, capacity, model_width)
    return (
        returned[0].reshape(out_shape),
        returned[1].reshape(out_shape),
        returned[2].reshape(out_shape),
        gate_grad.reshape(out_shape),
    )


def solution(mesh):
    in_specs = (
        P("dp", "seq", None, None),
        P("dp", "seq", None, None),
        P("dp", "seq", None, None),
        P("dp", "seq", None, None),
        P("dp", "seq", None, None),
        P("dp", "seq", None, None),
        P(None, "seq", None),
        P("dp"),
        P("dp", None, None),
    )
    out_specs = (
        P("dp", "seq", None, None),
        P("dp", "seq", None, None),
        P("dp", "seq", None, None),
        P("dp", "seq", None, None),
    )
    return jax.shard_map(local, mesh=mesh, in_specs=in_specs, out_specs=out_specs, check_vma=False)
```

profile of v0, /device:TPU:0, one launch (start us, length us, event | category | flops | bytes accessed | tf_op | source)
XLA Modules:
  0.0 369.2 jit_solution(3230899232040963151)
XLA Ops:
  8.8 2.2 multiply_reduce_fusion
  11.1 2.3 fusion.18
  13.9 1.9 fusion.15
  15.9 1.9 fusion.17
  17.8 21.0 %all_to_all.35 = bf16[16,24,1024]{2,1,0:T(8,128)(2,1)S(1)} all-to-all(bf16[16,24,1024]{2,1,0:T(8,128)(2,1)S(1)} %fusion.17), channel_id=1, replica_groups=mesh['dp'=16,'seq'=8] {'dp'}, dimensions={0} | all-to-all | bytes 1572864 | tf_op jit(solution)/shard_map/all_to_all | solution.py:82
  38.8 16.4 %all_to_all.36 = bf16[16,24,1024]{2,1,0:T(8,128)(2,1)S(1)} all-to-all(bf16[16,24,1024]{2,1,0:T(8,128)(2,1)S(1)} %bitcast.158), channel_id=1, replica_groups=mesh['dp'=16,'seq'=8] {'dp'}, dimensions={0} | all-to-all | bytes 1572864 | tf_op jit(solution)/shard_map/all_to_all | solution.py:76
  55.2 15.4 %all_to_all.37 = bf16[16,24,1024]{2,1,0:T(8,128)(2,1)S(1)} all-to-all(bf16[16,24,1024]{2,1,0:T(8,128)(2,1)} %bitcast.159), channel_id=1, replica_groups=mesh['dp'=16,'seq'=8] {'dp'}, dimensions={0} | all-to-all | bytes 1572864 | tf_op jit(solution)/shard_map/all_to_all | solution.py:79
  70.6 3.6 all-to-all-start.3
  74.7 2.0 gather_fusion.1
  76.7 2.0 gather_fusion
  79.8 5.9 %all-to-all-done.3 = bf16[16,24,1024]{2,1,0:T(8,128)(2,1)S(1)} async-done(((bf16[16,24,1024]{2,1,0:T(8,128)(2,1)}), bf16[16,24,1024]{2,1,0:T(8,128)(2,1)S(1)}, u32[]{:S(2)}, u32[]{:S(2)}) %all-to-all-start.3) | async-done | bytes 786464 | tf_op jit(solution)/shard_map/all_to_all | solution.py:73
  87.0 1.6 broadcast_select_fusion
  92.9 2.1 fusion.30
  95.0 2.1 fusion.33
  97.0 2.0 fusion.36
  99.0 2.1 fusion.39
  101.1 18.8 %all-gather.7.cloned.1.call-done = bf16[2048,1024]{1,0:T(8,128)(2,1)} async-done(((bf16[256,1024]{1,0:T(8,128)(2,1)}), bf16[2048,1024]{1,0:T(8,128)(2,1)}) %all-gather.7.cloned.1.call-update) | async-done | bytes 4194320 | tf_op jit(solution)/shard_map/all_gather | solution.py:130
  119.9 4.0 %fusion.111 = (bf16[1024,1024]{1,0:T(8,128)(2,1)}, bf16[1024,1024]{1,0:T(8,128)(2,1)S(1)}) fusion(bf16[2048,1024]{1,0:T(8,128)(2,1)} %all-gather.7.cloned.1.call-done), kind=kLoop, calls=%fused_computation.176 | loop fusion | bytes 8388608 | tf_op jit(solution)/shard_map/slice | solution.py:22
  124.0 2.8 copy.69
  126.8 27.6 %all-gather.9.cloned.1.call-done = bf16[2048,1024]{1,0:T(8,128)(2,1)} async-done(((bf16[256,1024]{1,0:T(8,128)(2,1)}), bf16[2048,1024]{1,0:T(8,128)(2,1)}) %all-gather.9.cloned.1.call-update) | async-done | bytes 4194320 | tf_op jit(solution)/shard_map/all_gather | solution.py:128
  154.4 4.0 %fusion.110 = (bf16[1024,1024]{1,0:T(8,128)(2,1)S(1)}, bf16[1024,1024]{1,0:T(8,128)(2,1)}) fusion(bf16[2048,1024]{1,0:T(8,128)(2,1)} %all-gather.9.cloned.1.call-done), kind=kLoop, calls=%fused_computation.175 | loop fusion | bytes 8388608 | tf_op jit(solution)/shard_map/slice | solution.py:22
  158.4 3.9 %copy.81 = bf16[1024,1024]{0,1:T(8,128)(2,1)} copy(bf16[1024,1024]{1,0:T(8,128)(2,1)} %get-tuple-element.15) | data formatting | bytes 4194304 | tf_op jit(solution)/shard_map/slice | solution.py:22
  162.4 26.5 %all-gather.11.cloned.1.call-done = bf16[2048,1024]{1,0:T(8,128)(2,1)} async-done(((bf16[256,1024]{1,0:T(8,128)(2,1)}), bf16[2048,1024]{1,0:T(8,128)(2,1)}) %all-gather.11.cloned.1.call-update) | async-done | bytes 4194320 | tf_op jit(solution)/shard_map/all_gather | solution.py:131
  188.9 4.7 %fusion.109 = (bf16[1024,1024]{1,0:T(8,128)(2,1)}, bf16[1024,1024]{1,0:T(8,128)(2,1)}) fusion(bf16[2048,1024]{1,0:T(8,128)(2,1)} %all-gather.11.cloned.1.call-done), kind=kLoop, calls=%fused_computation.174 | loop fusion | bytes 8388608 | tf_op jit(solution)/shard_map/slice | solution.py:22
  193.6 4.0 %copy.82 = bf16[1024,1024]{0,1:T(8,128)(2,1)} copy(bf16[1024,1024]{1,0:T(8,128)(2,1)} %get-tuple-element.13) | data formatting | bytes 4194304 | tf_op jit(solution)/shard_map/slice | solution.py:22
  197.6 6.3 %fusion.58 = f32[8,256,1024]{2,1,0:T(8,128)} fusion(bf16[1024,8,128]{0,2,1:T(8,128)(2,1)} %bitcast.140, bf16[256,1024]{1,0:T(8,128)(2,1)S(1)} %copy-done.5), kind=kOutput, calls=%fused_computation.83 | convolution fusion | flops 536870912 | bytes 11010048 | tf_op jit(solution)/shard_map/thd,shd->hts/dot_general | solution.py:33
  205.3 3.2 copy-done.1
  208.5 4.1 %fusion = f32[8,128,256]{2,1,0:T(8,128)} fusion(bf16[1024,8,128]{0,2,1:T(8,128)(2,1)S(1)} %bitcast.157, f32[8,1024,256]{2,1,0:T(8,128)S(1)} %fusion.46, f32[1024,256]{1,0:T(8,128)S(1)} %copy-done.16), kind=kOutput, calls=%fused_computation.15 | convolution fusion | flops 551550976 | bytes 12582912 | tf_op jit(solution)/shard_map/hts,thd->shd/dot_general | solution.py:45
  212.6 10.7 %fusion.4 = f32[8,128,256]{2,1,0:T(8,128)} fusion(bf16[1024,8,128]{0,2,1:T(8,128)(2,1)} %bitcast.141, f32[8,1024,256]{2,1,0:T(8,128)} %copy-done.1, f32[1024,256]{1,0:T(8,128)} %fusion.36, bf16[1024,8,128]{0,2,1:T(8,128)(2,1)} %bitcast.156, bf16[256,1024]{1,0:T(8,128)(2,1)} %get-tuple-element.32), kind=kOutput, calls=%fused_computation.19 | convolution fusion | flops 1096810496 | bytes 15204352 | tf_op jit(solution)/shard_map/hts,thd->shd/dot_general | solution.py:42
  223.3 4.8 %fusion.112 = (bf16[1024,1024]{1,0:T(8,128)(2,1)}, bf16[1024,1024]{1,0:T(8,128)(2,1)}) fusion(bf16[2048,1024]{1,0:T(8,128)(2,1)} %all-gather.5.cloned.1.call-done), kind=kLoop, calls=%fused_computation.177 | loop fusion | bytes 8388608 | tf_op jit(solution)/shard_map/slice | solution.py:22
  228.2 4.0 %copy.68 = bf16[1024,1024]{0,1:T(8,128)(2,1)} copy(bf16[1024,1024]{1,0:T(8,128)(2,1)} %get-tuple-element.19) | data formatting | bytes 4194304 | tf_op jit(solution)/shard_map/slice | solution.py:22
  232.1 4.3 %copy.75 = bf16[1024,1024]{0,1:T(8,128)(2,1)} copy(bf16[1024,1024]{1,0:T(8,128)(2,1)} %get-tuple-element.16) | data formatting | bytes 4194304 | tf_op jit(solution)/shard_map/slice | solution.py:22
  236.5 6.1 %fusion.56 = f32[8,256,1024]{2,1,0:T(8,128)} fusion(bf16[1024,8,128]{0,2,1:T(8,128)(2,1)} %bitcast.145, bf16[256,1024]{1,0:T(8,128)(2,1)S(1)} %copy-done.5), kind=kOutput, calls=%fused_computation.81 | convolution fusion | flops 536870912 | bytes 11010048 | tf_op jit(solution)/shard_map/thd,shd->hts/dot_general | solution.py:33
  242.5 4.0 %copy.74 = bf16[1024,1024]{0,1:T(8,128)(2,1)} copy(bf16[1024,1024]{1,0:T(8,128)(2,1)} %get-tuple-element.18) | data formatting | bytes 4194304 | tf_op jit(solution)/shard_map/slice | solution.py:22
  246.5 10.8 %fusion.2 = f32[8,128,256]{2,1,0:T(8,128)} fusion(bf16[1024,8,128]{0,2,1:T(8,128)(2,1)} %bitcast.154, f32[8,256,1024]{2,1,0:T(8,128)} %fusion.58, f32[256,1024]{1,0:T(8,128)} %fusion.30, bf16[256,1024]{1,0:T(8,128)(2,1)S(1)} %copy-done.11), kind=kOutput, calls=%fused_computation.17 | convolution fusion | flops 1096810496 | bytes 13107200 | tf_op jit(solution)/shard_map/hts,shd->thd/dot_general | solution.py:38
  257.3 10.8 %fusion.26 = bf16[8,128,256]{2,1,0:T(8,128)(2,1)} fusion(f32[8,128,256]{2,1,0:T(8,128)} %fusion.2, bf16[1024,8,128]{0,2,1:T(8,128)(2,1)} %bitcast.155, f32[8,256,1024]{2,1,0:T(8,128)} %fusion.56, f32[256,1024]{1,0:T(8,128)} %fusion.33, bf16[256,1024]{1,0:T(8,128)(2,1)S(1)} %copy-done.11), kind=kOutput, calls=%fused_computation.46 | convolution fusion | flops 1097596928 | bytes 13631488 | tf_op jit(solution)/shard_map/hts,shd->thd/dot_general | solution.py:38
  269.4 2.7 copy.87
  272.1 6.3 %fusion.44 = f32[8,1024,256]{2,1,0:T(8,128)} fusion(bf16[1024,8,128]{0,2,1:T(8,128)(2,1)} %bitcast.143, bf16[256,1024]{1,0:T(8,128)(2,1)S(1)} %copy-done.4), kind=kOutput, calls=%fused_computation.73 | convolution fusion | flops 536870912 | bytes 11010048 | tf_op jit(solution)/shard_map/thd,shd->hts/dot_general | solution.py:28
  278.4 2.6 copy.88
  281.0 9.7 %fusion.27 = bf16[8,128,256]{2,1,0:T(8,128)(2,1)S(1)} fusion(f32[8,128,256]{2,1,0:T(8,128)} %fusion.4, bf16[1024,8,128]{0,2,1:T(8,128)(2,1)} %bitcast.144, f32[8,1024,256]{2,1,0:T(8,128)} %fusion.44, f32[1024,256]{1,0:T(8,128)} %fusion.39, bf16[1024,8,128]{0,2,1:T(8,128)(2,1)} %bitcast.152, bf16[256,1024]{1,0:T(8,128)(2,1)S(1)} %copy-done.10), kind=kOutput, calls=%fused_computation.47 | convolution fusion | flops 1097596928 | bytes 15728640 | tf_op jit(solution)/shard_map/hts,thd->shd/dot_general | solution.py:42
  290.9 2.1 gather_fusion.4
  293.0 2.1 gather_fusion.5
  295.1 7.2 %fusion.25 = bf16[8,128,256]{2,1,0:T(8,128)(2,1)S(1)} fusion(f32[8,128,256]{2,1,0:T(8,128)} %fusion, bf16[1024,8,128]{0,2,1:T(8,128)(2,1)} %bitcast.153, f32[8,1024,256]{2,1,0:T(8,128)} %fusion.44, f32[1024,256]{1,0:T(8,128)} %fusion.39), kind=kOutput, calls=%fused_computation.45 | convolution fusion | flops 552075264 | bytes 13107200 | tf_op jit(solution)/shard_map/hts,thd->shd/dot_general | solution.py:45
  302.5 2.1 gather_fusion.6
  305.9 21.1 %all_to_all.38 = bf16[16,24,1024]{2,1,0:T(8,128)(2,1)S(1)} all-to-all(bf16[16,24,1024]{2,1,0:T(8,128)(2,1)S(1)} %bitcast.148), channel_id=1, replica_groups=mesh['dp'=16,'seq'=8] {'dp'}, dimensions={0} | all-to-all | bytes 1572864 | tf_op jit(solution)/shard_map/all_to_all | solution.py:160
  327.0 16.8 %all_to_all.39 = bf16[16,24,1024]{2,1,0:T(8,128)(2,1)S(1)} all-to-all(bf16[16,24,1024]{2,1,0:T(8,128)(2,1)S(1)} %bitcast.147), channel_id=1, replica_groups=mesh['dp'=16,'seq'=8] {'dp'}, dimensions={0} | all-to-all | bytes 1572864 | tf_op jit(solution)/shard_map/all_to_all | solution.py:161
  343.8 3.6 all-to-all-start.6
  347.5 12.4 %all-to-all-done.6 = bf16[16,24,1024]{2,1,0:T(8,128)(2,1)S(1)} async-done(((bf16[16,24,1024]{2,1,0:T(8,128)(2,1)}), bf16[16,24,1024]{2,1,0:T(8,128)(2,1)S(1)}, u32[]{:S(2)}, u32[]{:S(2)}) %all-to-all-start.6) | async-done | bytes 786464 | tf_op jit(solution)/shard_map/all_to_all | solution.py:162
  (87 shorter events, 15.4 us)
Async XLA Ops:
  7.2 6.6 %copy-start = (bf16[1,1,384,1024]{3,2,1,0:T(8,128)(2,1)S(1)}, bf16[1,1,384,1024]{3,2,1,0:T(8,128)(2,1)}, u32[]{:S(2)}) copy-start(bf16[1,1,384,1024]{3,2,1,0:T(8,128)(2,1)} %param.17) | copy-start | bytes 2359300
  7.2 6.6 %copy-start.7 = (bf16[1,1,384,1024]{3,2,1,0:T(8,128)(2,1)S(1)}, bf16[1,1,384,1024]{3,2,1,0:T(8,128)(2,1)}, u32[]{:S(2)}) copy-start(bf16[1,1,384,1024]{3,2,1,0:T(8,128)(2,1)} %param.16) | copy-start | bytes 2359300
  7.2 6.6 %copy-start.6 = (bf16[1,1,384,1024]{3,2,1,0:T(8,128)(2,1)S(1)}, bf16[1,1,384,1024]{3,2,1,0:T(8,128)(2,1)}, u32[]{:S(2)}) copy-start(bf16[1,1,384,1024]{3,2,1,0:T(8,128)(2,1)} %param.18) | copy-start | bytes 2359300
  7.2 6.3 %copy-start.14 = (s32[16,1,16]{2,1,0:T(1,128)S(1)}, s32[16,1,16]{2,1,0:T(1,128)}, u32[]{:S(2)}) copy-start(s32[16,1,16]{2,1,0:T(1,128)} %param.19) | copy-start | bytes 3076
  13.8 25.0 %copy-start.13 = (bf16[1,1,384,1024]{3,2,1,0:T(8,128)(2,1)S(1)}, bf16[1,1,384,1024]{3,2,1,0:T(8,128)(2,1)}, u32[]{:S(2)}) copy-start(bf16[1,1,384,1024]{3,2,1,0:T(8,128)(2,1)} %param.14) | copy-start | bytes 2359300
  70.6 15.1 %all-to-all-start.3 = ((bf16[16,24,1024]{2,1,0:T(8,128)(2,1)}), bf16[16,24,1024]{2,1,0:T(8,128)(2,1)S(1)}, u32[]{:S(2)}, u32[]{:S(2)}) async-start(bf16[16,24,1024]{2,1,0:T(8,128)(2,1)} %bitcast.160), calls=%async_computation.3 | async-start | bytes 1572864 | tf_op jit(solution)/shard_map/all_to_all | solution.py:73
  74.3 45.7 %all-gather.7.cloned.1.call-start = ((), (), s32[]{:S(2)}) async-start(), calls=%async_computation.8 | async-start | bytes 4718592 | tf_op jit(solution)/shard_map/all_gather | solution.py:130
  78.7 8.3 %copy-start.8 = (bf16[256,1024]{1,0:T(8,128)(2,1)S(1)}, bf16[256,1024]{1,0:T(8,128)(2,1)}, u32[]{:S(2)}) copy-start(bf16[256,1024]{1,0:T(8,128)(2,1)} %gather_fusion.1) | copy-start | bytes 1572868
  78.7 8.3 %copy-start.9 = (bf16[256,1024]{1,0:T(8,128)(2,1)S(1)}, bf16[256,1024]{1,0:T(8,128)(2,1)}, u32[]{:S(2)}) copy-start(bf16[256,1024]{1,0:T(8,128)(2,1)} %gather_fusion) | copy-start | bytes 1572868
  86.9 4.7 %copy-start.15 = (s32[1,16,16]{2,1,0:T(8,128)S(1)}, s32[1,16,16]{2,1,0:T(8,128)}, u32[]{:S(2)}) copy-start(s32[1,16,16]{2,1,0:T(8,128)} %param.21) | copy-start | bytes 3076
  88.6 65.8 %all-gather.9.cloned.1.call-start = ((), (), s32[]{:S(2)}) async-start(), calls=%async_computation.9 | async-start | bytes 4718592 | tf_op jit(solution)/shard_map/all_gather | solution.py:128
  89.3 99.5 %all-gather.11.cloned.1.call-start = ((), (), s32[]{:S(2)}) async-start(), calls=%async_computation.10 | async-start | bytes 4718592 | tf_op jit(solution)/shard_map/all_gather | solution.py:131
  90.0 133.3 %all-gather.5.cloned.1.call-start = ((), (), s32[]{:S(2)}) async-start(), calls=%async_computation.7 | async-start | bytes 4718592 | tf_op jit(solution)/shard_map/all_gather | solution.py:129
  193.6 4.0 %copy-start.5 = (bf16[256,1024]{1,0:T(8,128)(2,1)S(1)}, bf16[256,1024]{1,0:T(8,128)(2,1)}, u32[]{:S(2)}) copy-start(bf16[256,1024]{1,0:T(8,128)(2,1)} %get-tuple-element.31) | copy-start | bytes 1572868
  197.6 6.3 %copy-start.3 = (bf16[1024,1024]{0,1:T(8,128)(2,1)S(1)}, bf16[1024,1024]{0,1:T(8,128)(2,1)}, u32[]{:S(2)}) copy-start(bf16[1024,1024]{0,1:T(8,128)(2,1)} %copy.81) | copy-start | bytes 6291460
  197.6 6.3 %copy-start.4 = (bf16[256,1024]{1,0:T(8,128)(2,1)S(1)}, bf16[256,1024]{1,0:T(8,128)(2,1)}, u32[]{:S(2)}) copy-start(bf16[256,1024]{1,0:T(8,128)(2,1)} %get-tuple-element.33) | copy-start | bytes 1572868
  203.9 4.6 %copy-start.12 = (bf16[1024,1024]{0,1:T(8,128)(2,1)S(1)}, bf16[1024,1024]{0,1:T(8,128)(2,1)}, u32[]{:S(2)}) copy-start(bf16[1024,1024]{0,1:T(8,128)(2,1)} %copy.82) | copy-start | bytes 6291460
  203.9 4.6 %copy-start.16 = (f32[1024,256]{1,0:T(8,128)S(1)}, f32[1024,256]{1,0:T(8,128)}, u32[]{:S(2)}) copy-start(f32[1024,256]{1,0:T(8,128)} %fusion.36) | copy-start | bytes 3145732
  205.3 3.2 copy-start.1
  242.5 4.0 %copy-start.11 = (bf16[256,1024]{1,0:T(8,128)(2,1)S(1)}, bf16[256,1024]{1,0:T(8,128)(2,1)}, u32[]{:S(2)}) copy-start(bf16[256,1024]{1,0:T(8,128)(2,1)} %get-tuple-element.30) | copy-start | bytes 1572868
  272.1 6.3 %copy-start.2 = (bf16[1024,1024]{1,0:T(8,128)(2,1)S(1)}, bf16[1024,1024]{1,0:T(8,128)(2,1)}, u32[]{:S(2)}) copy-start(bf16[1024,1024]{1,0:T(8,128)(2,1)} %get-tuple-element.12) | copy-start | bytes 6291460
  278.4 2.7 copy-start.10
  343.8 16.0 %all-to-all-start.6 = ((bf16[16,24,1024]{2,1,0:T(8,128)(2,1)}), bf16[16,24,1024]{2,1,0:T(8,128)(2,1)S(1)}, u32[]{:S(2)}, u32[]{:S(2)}) async-start(bf16[16,24,1024]{2,1,0:T(8,128)(2,1)} %bitcast.33), calls=%async_computation.6 | async-start | bytes 1572864 | tf_op jit(solution)/shard_map/all_to_all | solution.py:162
Sparse Core Ops, SparseCore 0:
  88.7 31.2 all-gather.6
  122.2 32.1 all-gather.8
  156.7 32.1 all-gather.10
  190.4 32.1 all-gather.4
where the time goes:
time: 375 us; the launch traced here: 369 us
  waiting for transfers between devices  92.7 us (25%)
  blocking collectives  90.8 us (24%)
  matrix products  82.7 us (22%)
  local copies, waits for them, and re-layouts  66.8 us (18%)
  between operations  15 us (4%)
  other arithmetic  13.3 us (4%)
  starting transfers between devices  7.89 us (2%)
    slice x12, local copies, waits for them, and re-layouts, cut_rows(): return array[offset:offset + extent].reshape(extent, head_count, -1)  46 us
    all_gather x1, waiting for transfers between devices, local(): shard_query = lax.all_gather(history[0], 'seq', axis=0, tiled=True)  27.6 us
    all_gather x1, waiting for transfers between devices, local(): shard_grad = lax.all_gather(history[3], 'seq', axis=0, tiled=True)  26.5 us
    dot_general x2, matrix products, pair_terms(): jnp.einsum('hts,shd->thd', score_grad, key_rows, preferred_element_type=j...  21.6 us
    all_to_all x1, blocking collectives, local(): lax.all_to_all(pack(grads[0]), 'dp', split_axis=0, concat_axis=0, tiled=T...  21.1 us
    all_to_all x1, blocking collectives, local(): lax.all_to_all(attn_grad.reshape(shape_slots), 'dp', split_axis=0, concat...  21 us
    dot_general x2, matrix products, pair_terms(): jnp.einsum('hts,thd->shd', score_grad, query_rows, preferred_element_type...  20.4 us
    all_gather x1, waiting for transfers between devices, local(): shard_value = lax.all_gather(history[2], 'seq', axis=0, tiled=True)  18.8 us
  transfers between devices with their start and end apart: 6, of which 5 were waited for; matrix products, arithmetic and copies ran while one was open for 17% of the time, Pallas kernels for 0%

commit v1 on v0

--- a/solution.py
+++ b/solution.py
@@ -127,7 +127,9 @@
     anchor = jnp.int32(0)
     shard_query = lax.all_gather(history[0], "seq", axis=0, tiled=True)
     shard_key = lax.all_gather(history[1], "seq", axis=0, tiled=True)
-    shard_value = lax.all_gather(history[2], "seq", axis=0, tiled=True)
+    shard_value = jnp.concatenate(
+        lax.all_to_all(jnp.stack([history[2]] * lax.axis_size("seq")), "seq", 0, 0), axis=0
+    )
     shard_grad = lax.all_gather(history[3], "seq", axis=0, tiled=True)
     total = shard_query.shape[0]
     query_sum = zeros

time: 375 us -> 360 us (0.960)
  waiting for transfers between devices: 92.7 us -> 80.4 us
  starting transfers between devices: 7.89 us -> 13 us
  blocking collectives: 90.8 us -> 86.9 us
    all_to_all x0 -> x1, waiting for transfers between devices: none -> 61.3 us  [local(): lax.all_to_all(jnp.stack([history[2]] * lax.axis_size('seq')), 'seq', 0, 0)]
    all_gather x1, waiting for transfers between devices: 27.6 us -> 0.01 us  [local(): shard_query = lax.all_gather(history[0], 'seq', axis=0, tiled=True)]
    all_gather x1, waiting for transfers between devices: 26.5 us -> 0.01 us  [local(): shard_grad = lax.all_gather(history[3], 'seq', axis=0, tiled=True)]
    all_gather x1 -> x0, waiting for transfers between devices: 18.8 us -> none  [local(): shard_value = lax.all_gather(history[2], 'seq', axis=0, tiled=True)]
    slice x12 -> x10, local copies, waits for them, and re-layouts: 46 us -> 38.1 us  [cut_rows(): return array[offset:offset + extent].reshape(extent, head_count, -1)]
    all_to_all x0 -> x1, starting transfers between devices: none -> 5.45 us  [local(): lax.all_to_all(jnp.stack([history[2]] * lax.axis_size('seq')), 'seq', 0, 0)]
    all_to_all x1, blocking collectives: 21.1 us -> 17.1 us  [local(): lax.all_to_all(pack(grads[0]), 'dp', split_axis=0, concat_axis=0, tiled=T...]
  transfers between devices with their start and end apart: 6 -> 6, of which waited for: 5 -> 3; matrix products, arithmetic and copies ran while one was open for 17% -> 19% of each run, Pallas kernels for 0% -> 0%
where the time goes in v1:
time: 360 us; the launch traced here: 354 us
  blocking collectives  86.9 us (24%)
  matrix products  80.9 us (22%)
  waiting for transfers between devices  80.4 us (22%)
  local copies, waits for them, and re-layouts  63.5 us (18%)
  between operations  15 us (4%)
  other arithmetic  14.2 us (4%)
  starting transfers between devices  13 us (4%)
    all_to_all x1, waiting for transfers between devices, local(): lax.all_to_all(jnp.stack([history[2]] * lax.axis_size('seq')), 'seq', 0, 0)  61.3 us
    slice x10, local copies, waits for them, and re-layouts, cut_rows(): return array[offset:offset + extent].reshape(extent, head_count, -1)  38.1 us
    dot_general x2, matrix products, pair_terms(): jnp.einsum('hts,shd->thd', score_grad, key_rows, preferred_element_type=j...  21.6 us
    all_to_all x1, blocking collectives, local(): lax.all_to_all(attn_grad.reshape(shape_slots), 'dp', split_axis=0, concat...  21 us
    dot_general x2, matrix products, pair_terms(): jnp.einsum('hts,thd->shd', score_grad, query_rows, preferred_element_type...  20 us
    all_to_all x1, blocking collectives, local(): lax.all_to_all(pack(grads[0]), 'dp', split_axis=0, concat_axis=0, tiled=T...  17.1 us
    all_to_all x1, blocking collectives, local(): lax.all_to_all(pack(grads[1]), 'dp', split_axis=0, concat_axis=0, tiled=T...  16.9 us
    all_to_all x1, blocking collectives, local(): lax.all_to_all(flatten(keys).reshape(shape_slots), 'dp', split_axis=0, co...  16.4 us
  transfers between devices with their start and end apart: 6, of which 3 were waited for; matrix products, arithmetic and copies ran while one was open for 19% of the time, Pallas kernels for 0%

profile of v1, /device:TPU:0, one launch (start us, length us, event | category | flops | bytes accessed | tf_op | source)
XLA Modules:
  0.0 353.8 jit_solution(5749700005613973418)
XLA Ops:
  8.8 2.2 multiply_reduce_fusion
  11.1 2.3 fusion.22
  13.9 1.9 fusion.19
  15.9 1.9 fusion.21
  17.8 21.0 %all_to_all.40 = bf16[16,24,1024]{2,1,0:T(8,128)(2,1)S(1)} all-to-all(bf16[16,24,1024]{2,1,0:T(8,128)(2,1)S(1)} %fusion.21), channel_id=1, replica_groups=mesh['dp'=16,'seq'=8] {'dp'}, dimensions={0} | all-to-all | bytes 1572864 | tf_op jit(solution)/shard_map/all_to_all | solution.py:82
  38.8 16.4 %all_to_all.41 = bf16[16,24,1024]{2,1,0:T(8,128)(2,1)S(1)} all-to-all(bf16[16,24,1024]{2,1,0:T(8,128)(2,1)S(1)} %bitcast.162), channel_id=1, replica_groups=mesh['dp'=16,'seq'=8] {'dp'}, dimensions={0} | all-to-all | bytes 1572864 | tf_op jit(solution)/shard_map/all_to_all | solution.py:76
  55.2 15.4 %all_to_all.42 = bf16[16,24,1024]{2,1,0:T(8,128)(2,1)S(1)} all-to-all(bf16[16,24,1024]{2,1,0:T(8,128)(2,1)} %bitcast.163), channel_id=1, replica_groups=mesh['dp'=16,'seq'=8] {'dp'}, dimensions={0} | all-to-all | bytes 1572864 | tf_op jit(solution)/shard_map/all_to_all | solution.py:79
  70.6 3.6 %all-to-all-start.4 = ((bf16[16,24,1024]{2,1,0:T(8,128)(2,1)}), bf16[16,24,1024]{2,1,0:T(8,128)(2,1)S(1)}, u32[]{:S(2)}, u32[]{:S(2)}) async-start(bf16[16,24,1024]{2,1,0:T(8,128)(2,1)} %bitcast.164), calls=%async_computation.4 | async-start | bytes 1572864 | tf_op jit(solution)/shard_map/all_to_all | solution.py:73
  74.7 2.0 gather_fusion.1
  76.7 2.0 gather_fusion
  79.8 5.9 %all-to-all-done.4 = bf16[16,24,1024]{2,1,0:T(8,128)(2,1)S(1)} async-done(((bf16[16,24,1024]{2,1,0:T(8,128)(2,1)}), bf16[16,24,1024]{2,1,0:T(8,128)(2,1)S(1)}, u32[]{:S(2)}, u32[]{:S(2)}) %all-to-all-start.4) | async-done | bytes 786464 | tf_op jit(solution)/shard_map/all_to_all | solution.py:73
  85.7 2.0 gather_fusion.3
  87.7 2.4 broadcast_select_fusion
  90.9 2.5 stack.2
  93.5 5.4 %all-to-all-start.3 = ((bf16[8,256,1024]{2,1,0:T(8,128)(2,1)}), bf16[8,256,1024]{2,1,0:T(8,128)(2,1)}, u32[]{:S(2)}, u32[]{:S(2)}) async-start(bf16[8,256,1024]{2,1,0:T(8,128)(2,1)} %stack.2), calls=%async_computation.3 | async-start | bytes 8388608 | tf_op jit(solution)/shard_map/all_to_all | solution.py:131
  101.4 2.1 fusion.34
  103.6 2.1 fusion.37
  105.7 2.0 fusion.40
  107.7 2.0 fusion.43
  109.7 61.3 %all-to-all-done.3 = bf16[8,256,1024]{2,1,0:T(8,128)(2,1)} async-done(((bf16[8,256,1024]{2,1,0:T(8,128)(2,1)}), bf16[8,256,1024]{2,1,0:T(8,128)(2,1)}, u32[]{:S(2)}, u32[]{:S(2)}) %all-to-all-start.3) | async-done | bytes 4194336 | tf_op jit(solution)/shard_map/all_to_all | solution.py:131
  171.1 2.7 fusion.113
  175.1 4.5 %fusion.16 = f32[8,256,1024]{2,1,0:T(8,128)} fusion(bf16[1024,8,128]{2,1,0:T(8,128)(2,1)S(1)} %bitcast.147, bf16[256,1024]{1,0:T(8,128)(2,1)S(1)} %copy-done.4), kind=kOutput, calls=%fused_computation.29 | convolution fusion | flops 536870912 | bytes 11010048 | tf_op jit(solution)/shard_map/thd,shd->hts/dot_general | solution.py:33
  179.6 4.5 %fusion.14 = f32[8,256,1024]{2,1,0:T(8,128)} fusion(bf16[1024,8,128]{2,1,0:T(8,128)(2,1)S(1)} %bitcast.149, bf16[256,1024]{1,0:T(8,128)(2,1)S(1)} %copy-done.4), kind=kOutput, calls=%fused_computation.27 | convolution fusion | flops 536870912 | bytes 11010048 | tf_op jit(solution)/shard_map/thd,shd->hts/dot_general | solution.py:33
  184.1 4.0 %fusion.112 = (bf16[1024,1024]{1,0:T(8,128)(2,1)S(1)}, bf16[1024,1024]{1,0:T(8,128)(2,1)}) fusion(bf16[2048,1024]{1,0:T(8,128)(2,1)} %all-gather.6.cloned.1.call-done), kind=kLoop, calls=%fused_computation.177 | loop fusion | bytes 8388608 | tf_op jit(solution)/shard_map/slice | solution.py:22
  188.1 4.2 %copy.79 = bf16[1024,1024]{0,1:T(8,128)(2,1)} copy(bf16[1024,1024]{1,0:T(8,128)(2,1)} %get-tuple-element.15) | data formatting | bytes 4194304 | tf_op jit(solution)/shard_map/slice | solution.py:22
  192.3 4.9 %fusion.111 = (bf16[1024,1024]{1,0:T(8,128)(2,1)}, bf16[1024,1024]{1,0:T(8,128)(2,1)}) fusion(bf16[2048,1024]{1,0:T(8,128)(2,1)} %all-gather.8.cloned.1.call-done), kind=kLoop, calls=%fused_computation.176 | loop fusion | bytes 8388608 | tf_op jit(solution)/shard_map/slice | solution.py:22
  197.2 4.0 %copy.80 = bf16[1024,1024]{0,1:T(8,128)(2,1)} copy(bf16[1024,1024]{1,0:T(8,128)(2,1)} %get-tuple-element.13) | data formatting | bytes 4194304 | tf_op jit(solution)/shard_map/slice | solution.py:22
  201.2 3.1 fusion.50
  204.3 3.2 copy-done.1
  207.5 4.1 %fusion = f32[8,128,256]{2,1,0:T(8,128)} fusion(bf16[1024,8,128]{0,2,1:T(8,128)(2,1)S(1)} %bitcast.161, f32[8,1024,256]{2,1,0:T(8,128)S(1)} %fusion.50, f32[1024,256]{1,0:T(8,128)S(1)} %copy-done.17), kind=kOutput, calls=%fused_computation.15 | convolution fusion | flops 551550976 | bytes 12582912 | tf_op jit(solution)/shard_map/hts,thd->shd/dot_general | solution.py:45
  211.7 10.4 %fusion.4 = f32[8,128,256]{2,1,0:T(8,128)} fusion(bf16[1024,8,128]{0,2,1:T(8,128)(2,1)} %bitcast.143, f32[8,1024,256]{2,1,0:T(8,128)} %copy-done.1, f32[1024,256]{1,0:T(8,128)} %fusion.40, bf16[1024,8,128]{0,2,1:T(8,128)(2,1)} %bitcast.160, bf16[256,1024]{1,0:T(8,128)(2,1)S(1)} %copy-done.8), kind=kOutput, calls=%fused_computation.19 | convolution fusion | flops 1096810496 | bytes 15204352 | tf_op jit(solution)/shard_map/hts,thd->shd/dot_general | solution.py:42
  222.0 4.6 %fusion.114 = (bf16[1024,1024]{1,0:T(8,128)(2,1)}, bf16[1024,1024]{1,0:T(8,128)(2,1)}) fusion(bf16[2048,1024]{1,0:T(8,128)(2,1)} %all-gather.4.cloned.1.call-done), kind=kLoop, calls=%fused_computation.179 | loop fusion | bytes 8388608 | tf_op jit(solution)/shard_map/slice | solution.py:22
  226.7 4.0 %copy.68 = bf16[1024,1024]{0,1:T(8,128)(2,1)} copy(bf16[1024,1024]{1,0:T(8,128)(2,1)} %get-tuple-element.19) | data formatting | bytes 4194304 | tf_op jit(solution)/shard_map/slice | solution.py:22
  230.7 4.3 %copy.73 = bf16[1024,1024]{0,1:T(8,128)(2,1)} copy(bf16[1024,1024]{1,0:T(8,128)(2,1)} %get-tuple-element.18) | data formatting | bytes 4194304 | tf_op jit(solution)/shard_map/slice | solution.py:22
  235.0 10.8 %fusion.2 = f32[8,128,256]{2,1,0:T(8,128)} fusion(bf16[1024,8,128]{0,2,1:T(8,128)(2,1)} %bitcast.159, f32[8,256,1024]{2,1,0:T(8,128)} %fusion.16, f32[256,1024]{1,0:T(8,128)} %fusion.34, bf16[256,1024]{1,0:T(8,128)(2,1)S(1)} %copy-done.12), kind=kOutput, calls=%fused_computation.17 | convolution fusion | flops 1096810496 | bytes 13107200 | tf_op jit(solution)/shard_map/hts,shd->thd/dot_general | solution.py:38
  245.8 10.8 %fusion.30 = bf16[8,128,256]{2,1,0:T(8,128)(2,1)} fusion(f32[8,128,256]{2,1,0:T(8,128)} %fusion.2, bf16[1024,8,128]{0,2,1:T(8,128)(2,1)} %bitcast.158, f32[8,256,1024]{2,1,0:T(8,128)} %fusion.14, f32[256,1024]{1,0:T(8,128)} %fusion.37, bf16[256,1024]{1,0:T(8,128)(2,1)S(1)} %copy-done.12), kind=kOutput, calls=%fused_computation.50 | convolution fusion | flops 1097596928 | bytes 13631488 | tf_op jit(solution)/shard_map/hts,shd->thd/dot_general | solution.py:38
  257.9 2.6 copy.85
  260.4 6.3 %fusion.48 = f32[8,1024,256]{2,1,0:T(8,128)} fusion(bf16[1024,8,128]{0,2,1:T(8,128)(2,1)} %bitcast.144, bf16[256,1024]{1,0:T(8,128)(2,1)S(1)} %copy-done.3), kind=kOutput, calls=%fused_computation.77 | convolution fusion | flops 536870912 | bytes 11010048 | tf_op jit(solution)/shard_map/thd,shd->hts/dot_general | solution.py:28
  266.7 2.8 copy.86
  269.5 9.7 %fusion.31 = bf16[8,128,256]{2,1,0:T(8,128)(2,1)S(1)} fusion(f32[8,128,256]{2,1,0:T(8,128)} %fusion.4, bf16[1024,8,128]{0,2,1:T(8,128)(2,1)} %bitcast.145, f32[8,1024,256]{2,1,0:T(8,128)} %fusion.48, f32[1024,256]{1,0:T(8,128)} %fusion.43, bf16[1024,8,128]{0,2,1:T(8,128)(2,1)} %bitcast.156, bf16[256,1024]{1,0:T(8,128)(2,1)S(1)} %copy-done.9), kind=kOutput, calls=%fused_computation.51 | convolution fusion | flops 1097596928 | bytes 15728640 | tf_op jit(solution)/shard_map/hts,thd->shd/dot_general | solution.py:42
  279.4 2.1 gather_fusion.4
  281.5 2.1 gather_fusion.5
  283.6 7.2 %fusion.29 = bf16[8,128,256]{2,1,0:T(8,128)(2,1)S(1)} fusion(f32[8,128,256]{2,1,0:T(8,128)} %fusion, bf16[1024,8,128]{0,2,1:T(8,128)(2,1)} %bitcast.157, f32[8,1024,256]{2,1,0:T(8,128)} %fusion.48, f32[1024,256]{1,0:T(8,128)} %fusion.43), kind=kOutput, calls=%fused_computation.49 | convolution fusion | flops 552075264 | bytes 13107200 | tf_op jit(solution)/shard_map/hts,thd->shd/dot_general | solution.py:45
  291.0 2.1 gather_fusion.6
  294.4 17.1 %all_to_all.43 = bf16[16,24,1024]{2,1,0:T(8,128)(2,1)S(1)} all-to-all(bf16[16,24,1024]{2,1,0:T(8,128)(2,1)S(1)} %bitcast.152), channel_id=1, replica_groups=mesh['dp'=16,'seq'=8] {'dp'}, dimensions={0} | all-to-all | bytes 1572864 | tf_op jit(solution)/shard_map/all_to_all | solution.py:162
  311.5 16.9 %all_to_all.44 = bf16[16,24,1024]{2,1,0:T(8,128)(2,1)S(1)} all-to-all(bf16[16,24,1024]{2,1,0:T(8,128)(2,1)S(1)} %bitcast.151), channel_id=1, replica_groups=mesh['dp'=16,'seq'=8] {'dp'}, dimensions={0} | all-to-all | bytes 1572864 | tf_op jit(solution)/shard_map/all_to_all | solution.py:163
  328.4 3.6 %all-to-all-start.7 = ((bf16[16,24,1024]{2,1,0:T(8,128)(2,1)}), bf16[16,24,1024]{2,1,0:T(8,128)(2,1)S(1)}, u32[]{:S(2)}, u32[]{:S(2)}) async-start(bf16[16,24,1024]{2,1,0:T(8,128)(2,1)} %bitcast.31), calls=%async_computation.7 | async-start | bytes 1572864 | tf_op jit(solution)/shard_map/all_to_all | solution.py:164
  332.0 12.4 %all-to-all-done.7 = bf16[16,24,1024]{2,1,0:T(8,128)(2,1)S(1)} async-done(((bf16[16,24,1024]{2,1,0:T(8,128)(2,1)}), bf16[16,24,1024]{2,1,0:T(8,128)(2,1)S(1)}, u32[]{:S(2)}, u32[]{:S(2)}) %all-to-all-start.7) | async-done | bytes 786464 | tf_op jit(solution)/shard_map/all_to_all | solution.py:164
  (89 shorter events, 13.2 us)
Async XLA Ops:
  7.2 6.6 %copy-start = (bf16[1,1,384,1024]{3,2,1,0:T(8,128)(2,1)S(1)}, bf16[1,1,384,1024]{3,2,1,0:T(8,128)(2,1)}, u32[]{:S(2)}) copy-start(bf16[1,1,384,1024]{3,2,1,0:T(8,128)(2,1)} %param.17) | copy-start | bytes 2359300
  7.2 6.6 %copy-start.6 = (bf16[1,1,384,1024]{3,2,1,0:T(8,128)(2,1)S(1)}, bf16[1,1,384,1024]{3,2,1,0:T(8,128)(2,1)}, u32[]{:S(2)}) copy-start(bf16[1,1,384,1024]{3,2,1,0:T(8,128)(2,1)} %param.16) | copy-start | bytes 2359300
  7.2 6.6 %copy-start.5 = (bf16[1,1,384,1024]{3,2,1,0:T(8,128)(2,1)S(1)}, bf16[1,1,384,1024]{3,2,1,0:T(8,128)(2,1)}, u32[]{:S(2)}) copy-start(bf16[1,1,384,1024]{3,2,1,0:T(8,128)(2,1)} %param.18) | copy-start | bytes 2359300
  7.2 6.3 %copy-start.15 = (s32[16,1,16]{2,1,0:T(1,128)S(1)}, s32[16,1,16]{2,1,0:T(1,128)}, u32[]{:S(2)}) copy-start(s32[16,1,16]{2,1,0:T(1,128)} %param.19) | copy-start | bytes 3076
  13.8 25.0 %copy-start.14 = (bf16[1,1,384,1024]{3,2,1,0:T(8,128)(2,1)S(1)}, bf16[1,1,384,1024]{3,2,1,0:T(8,128)(2,1)}, u32[]{:S(2)}) copy-start(bf16[1,1,384,1024]{3,2,1,0:T(8,128)(2,1)} %param.14) | copy-start | bytes 2359300
  70.6 15.1 %all-to-all-start.4 = ((bf16[16,24,1024]{2,1,0:T(8,128)(2,1)}), bf16[16,24,1024]{2,1,0:T(8,128)(2,1)S(1)}, u32[]{:S(2)}, u32[]{:S(2)}) async-start(bf16[16,24,1024]{2,1,0:T(8,128)(2,1)} %bitcast.164), calls=%async_computation.4 | async-start | bytes 1572864 | tf_op jit(solution)/shard_map/all_to_all | solution.py:73
  74.3 109.9 %all-gather.6.cloned.1.call-start = ((), (), s32[]{:S(2)}) async-start(), calls=%async_computation.9 | async-start | bytes 4718592 | tf_op jit(solution)/shard_map/all_gather | solution.py:128
  78.7 9.0 %copy-start.10 = (bf16[256,1024]{1,0:T(8,128)(2,1)S(1)}, bf16[256,1024]{1,0:T(8,128)(2,1)}, u32[]{:S(2)}) copy-start(bf16[256,1024]{1,0:T(8,128)(2,1)} %gather_fusion.1) | copy-start | bytes 1572868
  78.7 9.0 %copy-start.11 = (bf16[256,1024]{1,0:T(8,128)(2,1)S(1)}, bf16[256,1024]{1,0:T(8,128)(2,1)}, u32[]{:S(2)}) copy-start(bf16[256,1024]{1,0:T(8,128)(2,1)} %gather_fusion) | copy-start | bytes 1572868
  90.1 3.3 copy-start.7
  90.2 102.2 %all-gather.8.cloned.1.call-start = ((), (), s32[]{:S(2)}) async-start(), calls=%async_computation.10 | async-start | bytes 4718592 | tf_op jit(solution)/shard_map/all_gather | solution.py:133
  93.4 6.7 %copy-start.16 = (s32[1,16,16]{2,1,0:T(8,128)S(1)}, s32[1,16,16]{2,1,0:T(8,128)}, u32[]{:S(2)}) copy-start(s32[1,16,16]{2,1,0:T(8,128)} %param.21) | copy-start | bytes 3076
  93.5 77.6 %all-to-all-start.3 = ((bf16[8,256,1024]{2,1,0:T(8,128)(2,1)}), bf16[8,256,1024]{2,1,0:T(8,128)(2,1)}, u32[]{:S(2)}, u32[]{:S(2)}) async-start(bf16[8,256,1024]{2,1,0:T(8,128)(2,1)} %stack.2), calls=%async_computation.3 | async-start | bytes 8388608 | tf_op jit(solution)/shard_map/all_to_all | solution.py:131
  98.9 123.1 %all-gather.4.cloned.1.call-start = ((), (), s32[]{:S(2)}) async-start(), calls=%async_computation.8 | async-start | bytes 4718592 | tf_op jit(solution)/shard_map/all_gather | solution.py:129
  173.8 1.3 copy-start.4
  197.2 4.0 %copy-start.3 = (bf16[256,1024]{1,0:T(8,128)(2,1)S(1)}, bf16[256,1024]{1,0:T(8,128)(2,1)}, u32[]{:S(2)}) copy-start(bf16[256,1024]{1,0:T(8,128)(2,1)} %get-tuple-element.33) | copy-start | bytes 1572868
  201.2 6.3 %copy-start.13 = (bf16[1024,1024]{0,1:T(8,128)(2,1)S(1)}, bf16[1024,1024]{0,1:T(8,128)(2,1)}, u32[]{:S(2)}) copy-start(bf16[1024,1024]{0,1:T(8,128)(2,1)} %copy.80) | copy-start | bytes 6291460
  201.2 6.3 %copy-start.17 = (f32[1024,256]{1,0:T(8,128)S(1)}, f32[1024,256]{1,0:T(8,128)}, u32[]{:S(2)}) copy-start(f32[1024,256]{1,0:T(8,128)} %fusion.40) | copy-start | bytes 3145732
  204.3 3.2 copy-start.1
  207.5 4.1 %copy-start.8 = (bf16[256,1024]{1,0:T(8,128)(2,1)S(1)}, bf16[256,1024]{1,0:T(8,128)(2,1)}, u32[]{:S(2)}) copy-start(bf16[256,1024]{1,0:T(8,128)(2,1)} %copy-done.7) | copy-start | bytes 1572868
  226.7 8.3 %copy-start.12 = (bf16[256,1024]{1,0:T(8,128)(2,1)S(1)}, bf16[256,1024]{1,0:T(8,128)(2,1)}, u32[]{:S(2)}) copy-start(bf16[256,1024]{1,0:T(8,128)(2,1)} %get-tuple-element.30) | copy-start | bytes 1572868
  260.4 6.3 %copy-start.2 = (bf16[1024,1024]{1,0:T(8,128)(2,1)S(1)}, bf16[1024,1024]{1,0:T(8,128)(2,1)}, u32[]{:S(2)}) copy-start(bf16[1024,1024]{1,0:T(8,128)(2,1)} %get-tuple-element.12) | copy-start | bytes 6291460
  266.7 2.8 copy-start.9
  328.4 16.1 %all-to-all-start.7 = ((bf16[16,24,1024]{2,1,0:T(8,128)(2,1)}), bf16[16,24,1024]{2,1,0:T(8,128)(2,1)S(1)}, u32[]{:S(2)}, u32[]{:S(2)}) async-start(bf16[16,24,1024]{2,1,0:T(8,128)(2,1)} %bitcast.31), calls=%async_computation.7 | async-start | bytes 1572864 | tf_op jit(solution)/shard_map/all_to_all | solution.py:164
Sparse Core Ops, SparseCore 0:
  90.3 53.6 all-gather.5
  146.3 37.1 all-gather.7
  185.8 28.6 all-gather.3
